TPU v7x, 32 devices: a whole 2x2x4 slice. The times are simulated.
32 devices in a mesh: grp: 8 (over z, x), sub: 4 (over y, core).
Axes of the slice: x: 2, y: 2, z: 4, core: 2. Of those that a mesh axis runs over, the one named last changes fastest.
Arguments:
- load: float32 [8, 4, 15, 384], P('grp', 'sub'), may hold values from -6 to 6
- couple: bfloat16 [8, 4, 4, 15, 15, 384], P('grp', 'sub'), may hold values from -1 to 6
- face_link: int32 [8, 4, 3, 384], P('grp', 'sub'), may hold values from 0 to 383, as said below
- face_count: int32 [8, 4], P('grp', 'sub'), may hold values from 192 to 384, as said below
- slot_face: int32 [8, 4, 4, 32], P('grp', 'sub'), may hold values from 0 to 383, as said below
- pair_count: int32 [8, 4, 4], P('grp', 'sub'), may hold values from 0 to 32, as said below
- basis: float32 [8, 4, 64, 15, 384], P('grp', 'sub'), may hold values from -0.0390625 to 0.0390625
- coarse_inverse: float32 [8, 4, 64, 64], P('grp', 'sub'), may hold values from -0.25 to 1.65
- coarse_block: float32 [8, 4, 6, 64, 64], P('grp', 'sub'), may hold values from -0.15625 to 0.15625
- coarse_link: int32 [8, 4, 6], P('grp', 'sub'), may hold values from 0 to 31, as said below
Outputs:
- trace_field: float32 [8, 4, 15, 384], P('grp', 'sub')
- robin_data: float32 [8, 4, 15, 384], P('grp', 'sub')
- coarse_coef: float32 [8, 4, 64], P('grp', 'sub')
Inputs may be any that keep to these rules, and one draw needn't show every extreme that they name: Subdomain (g, i) has live face blocks 0 to face_count[g, i] - 1; the rest are padding. Some subdomain has all 384 live. pair_count[g, i, j] equals pair_count[g, j, i], is 0 for j = i and otherwise 1 or more, a quarter of 32 or more, rounded down; every subdomain has exactly one peer with 32, and all its other peers have half of 32 or fewer. `slot_face`: for c < pair_count[g, i, j], slot c toward j names a live face block of i that i shares with j, the same face that slot c of j toward i names on j's side; these faces are distinct within a subdomain. Other slots name any face block. `face_link`: linked face blocks are live and differ from the face block itself. `coarse_link`: the 6 coarse neighbours of subdomain (g, i) are distinct, differ from it, and lie in groups g - 1, g or g + 1.
All inputs are finite; a program needn't handle non-finite values.
Results may differ from a plain program's by a relative error of at most 0.0015.
Values sent between devices are 32-bit elements; how exact they have to be, the bound alone decides.
A program may use at most 64 MiB of HBM per device.

v0:
```python
import functools

import jax
import jax.numpy as jnp
from jax import lax
from jax.experimental import pallas as pl
from jax.experimental.pallas import tpu as pltpu
from jax.sharding import PartitionSpec as P

ITERS = 3
SWEEPS = 2
CSWEEPS = 2
LANES = 128

robin_weight = 1.0
omega_step = 0.2
highest = lax.Precision.HIGHEST
MESH = pl.DeviceIdType.MESH


def pick_lanes(field, index):
    rows = field.shape[0]
    parts = []
    for d in range(index.shape[1] // LANES):
        wanted = jnp.broadcast_to(index[:, d * LANES : (d + 1) * LANES], (rows, LANES))
        within = wanted & (LANES - 1)
        chunk = wanted >> (LANES.bit_length() - 1)
        out = None
        for s in range(field.shape[1] // LANES):
            got = jnp.take_along_axis(
                field[:, s * LANES : (s + 1) * LANES], within, axis=1, mode="promise_in_bounds"
            )
            out = got if out is None else jnp.where(chunk == s, got, out)
        parts.append(out)
    return jnp.concatenate(parts, axis=1) if len(parts) > 1 else parts[0]


def iota(shape, dim):
    return lax.broadcasted_iota(jnp.int32, shape, dim)


def kernel(
    groups,
    peers,
    load_hbm,
    couple_hbm,
    link_hbm,
    count_hbm,
    slot_hbm,
    pair_hbm,
    basis_hbm,
    inverse_hbm,
    block_hbm,
    coarse_link_hbm,
    trace_out,
    robin_out,
    coef_out,
    load_ref,
    couple_ref,
    link_ref,
    count_ref,
    slot_ref,
    pair_ref,
    basis_ref,
    inverse_ref,
    block_ref,
    coarse_link_ref,
    load_s,
    trace_s,
    robin_s,
    stack_s,
    couple_s,
    moved_s,
    kept_s,
    table_s,
    folded_s,
    slots_s,
    inside_s,
    owner_s,
    interface_s,
    start_s,
    coarse_send,
    coarse_recv,
    robin_send,
    robin_recv,
    coarse_send_sem,
    coarse_recv_sem,
    robin_send_sem,
    robin_recv_sem,
    input_sem,
):
    g, me = lax.axis_index("grp"), lax.axis_index("sub")
    trace_dim, faces = load_ref.shape[1], load_ref.shape[-1]
    rows = load_s.shape[0]
    cvec = inverse_ref.shape[-1]
    links = link_ref.shape[1]
    kc = coarse_link_ref.shape[-1]
    cap = slot_ref.shape[-1]
    slot_lanes = peers * cap

    def per_group(act):
        @pl.when(g > 0)
        def _():
            act(-1)

        @pl.when(g < groups - 1)
        def _():
            act(1)

        act(0)

    def targets(d):
        first = 1 if d == 0 else 0
        return [(g + d, lax.rem(me + off, peers)) for off in range(first, peers)]

    operands = (
        (count_hbm, count_ref),
        (load_hbm, load_ref),
        (link_hbm, link_ref),
        (slot_hbm, slot_ref),
        (pair_hbm, pair_ref),
        (couple_hbm, couple_ref),
        (inverse_hbm, inverse_ref),
        (basis_hbm, basis_ref),
        (block_hbm, block_ref),
        (coarse_link_hbm, coarse_link_ref),
    )
    fetches = [
        pltpu.make_async_copy(src, dst, input_sem.at[i]) for i, (src, dst) in enumerate(operands)
    ]
    for fetch in fetches:
        fetch.start()
    barrier = pltpu.get_barrier_semaphore()

    def greet(d):
        for device in targets(d):
            pl.semaphore_signal(barrier, inc=1, device_id=device, device_id_type=MESH)

    per_group(greet)

    for fetch in fetches[:5]:
        fetch.wait()
    live = (iota((1, faces), 1) < count_ref[0, 0]).astype(jnp.float32)
    load_s[...] = jnp.zeros_like(load_s)
    for a in range(trace_dim):
        load_s[a : a + 1, :] = load_ref[0, a] * live
    moved_s[...] = jnp.zeros_like(moved_s)

    def unpack(b, carry):
        for s in range(faces // LANES):
            for k in range(links + 1):
                couple_s[s, b, (k + 1) * rows - 8 : (k + 1) * rows, :] = jnp.zeros((8, LANES), jnp.float32)
        for a in range(trace_dim):
            blocks = couple_ref[0, 0, a, b].astype(jnp.float32)
            for s in range(faces // LANES):
                couple_s[s, b, pl.ds(a, links + 1, stride=rows), :] = blocks[:, s * LANES : (s + 1) * LANES]
        return carry

    coarse_send[...] = jnp.zeros_like(coarse_send)
    slots_s[...] = jnp.zeros_like(slots_s)
    inside = jnp.zeros((1, faces), jnp.float32)
    owner = jnp.full((1, faces), -1.0, jnp.float32)
    eye_slots = iota((cap, cap), 0) == iota((cap, cap), 1)
    face_ids = iota((cap, faces), 1).astype(jnp.float32)
    place = iota((cap, faces), 0)
    for j in range(peers):
        slot_row = slot_ref[0, 0, j : j + 1, :]
        slots_s[:, j * cap : (j + 1) * cap] = slot_row
        as_float = jnp.broadcast_to(slot_row.astype(jnp.float32), (cap, cap))
        column = jnp.sum(jnp.where(eye_slots, as_float, 0.0), axis=1, keepdims=True)
        hit = (column == face_ids) & (place < pair_ref[0, 0, j])
        found = jnp.max(jnp.where(hit, place.astype(jnp.float32), -1.0), axis=0, keepdims=True)
        inside = jnp.where(found >= 0.0, found, inside)
        owner = jnp.where(found >= 0.0, float(j), owner)
    interface_s[...] = jnp.where(owner >= 0.0, 1.0, 0.0)
    inside_s[...] = inside.astype(jnp.int32)
    owner_s[...] = owner.astype(jnp.int32)
    robin_s[...] = jnp.zeros_like(robin_s)
    trace_s[...] = omega_step * load_s[...]
    eye = iota((cvec, cvec), 0) == iota((cvec, cvec), 1)

    fetches[5].wait()
    lax.fori_loop(0, trace_dim, unpack, 0)
    def apply(x):
        stack_s[0] = x
        for k in range(links):
            stack_s[k + 1] = pick_lanes(x, link_ref[0, k])
        chunks = []
        for s in range(faces // LANES):
            lanes = slice(s * LANES, (s + 1) * LANES)
            totals = []
            for k in range(links + 1):
                total = None
                for b in range(trace_dim):
                    term = couple_s[s, b, k * rows : (k + 1) * rows, :] * stack_s[k, b : b + 1, lanes]
                    total = term if total is None else total + term
                totals.append(total)
            chunks.append(functools.reduce(jnp.add, totals))
        product = jnp.concatenate(chunks, axis=1)
        return live * (product + robin_weight * interface_s[...] * x)

    def right_side():
        return load_s[...] + live * robin_s[...]

    def sweep(x, bx):
        return x + omega_step * (right_side() - bx)

    def as_row(column):
        return jnp.sum(jnp.where(eye, column, 0.0), axis=0, keepdims=True)

    def send_row(t, r, row):
        coarse_send[t, r, :, 0:cvec] = row

        def push(d):
            for device in targets(d):
                pltpu.make_async_remote_copy(
                    src_ref=coarse_send.at[t, r],
                    dst_ref=coarse_recv.at[t, r, (1 - d) * peers + me],
                    send_sem=coarse_send_sem.at[t, r, 1 + d],
                    recv_sem=coarse_recv_sem.at[t, r, 1 - d],
                    device_id=device,
                    device_id_type=MESH,
                ).start()

        per_group(push)

    def wait_rows(t, r, sems):
        def wait(d):
            n = peers - 1 if d == 0 else peers
            part = coarse_recv.at[t, r, pl.ds((1 + d) * peers, n)]
            pltpu.make_async_copy(part, part, sems.at[t, r, 1 + d]).wait()

        per_group(wait)

    def coupled(t, r):
        table_s[...] = coarse_recv[t, r]
        total = None
        for k in range(kc):
            position = coarse_link_ref[0, 0, k] - (g - 1) * peers
            position = jnp.minimum(jnp.maximum(position, 0), 3 * peers - 1)
            term = folded_s[k] * table_s[position][:, 0:cvec]
            total = term if total is None else total + term
        return jnp.sum(total, axis=1, keepdims=True)

    def robin_copy(t, off):
        to = lax.rem(me + off, peers)
        chunk = lax.div(to * cap, LANES)
        return pltpu.make_async_remote_copy(
            src_ref=robin_send.at[t, chunk],
            dst_ref=robin_recv.at[t, off - 1],
            send_sem=robin_send_sem.at[t, off - 1],
            recv_sem=robin_recv_sem.at[t, off - 1],
            device_id=(g, to),
            device_id_type=MESH,
        )

    def front():
        x = trace_s[...]
        for _ in range(SWEEPS - 1):
            x = sweep(x, apply(x))
        residual = right_side() - apply(x)
        trace_s[...] = x
        part = jnp.zeros((cvec, LANES), jnp.float32)
        for a in range(trace_dim):
            product = basis_ref[0, 0, a] * residual[a : a + 1, :]
            for s in range(faces // LANES):
                part = part + product[:, s * LANES : (s + 1) * LANES]
        restricted = jnp.sum(part, axis=1, keepdims=True)
        start = jnp.sum(inverse_ref[0, 0] * as_row(restricted), axis=1, keepdims=True)
        start_s[...] = jnp.broadcast_to(start, start_s.shape)

    def fold():
        for k in range(kc):
            folded_s[k] = jnp.dot(
                inverse_ref[0, 0],
                block_ref[0, 0, k],
                precision=highest,
                preferred_element_type=jnp.float32,
            )

    for fetch in fetches[6:]:
        fetch.wait()
    front()
    count = (peers - 1) + jnp.where(g > 0, peers, 0) + jnp.where(g < groups - 1, peers, 0)
    pl.semaphore_wait(barrier, count)

    def iteration(t, carry):
        start = start_s[:, 0:1]
        coef = start
        for r in range(CSWEEPS):
            send_row(t, r, as_row(coef))
            if r == 0:
                pl.when(t == 0)(fold)
            wait_rows(t, r, coarse_recv_sem)
            coef = start - coupled(t, r)
        coef_out[0] = as_row(coef)
        wide = jnp.broadcast_to(coef, (cvec, faces))
        for a in range(trace_dim):
            moved_s[a : a + 1, :] = jnp.sum(basis_ref[0, 0, a] * wide, axis=0, keepdims=True)
        x = trace_s[...] + live * moved_s[...]
        kept_s[...] = x
        outgoing = 2.0 * robin_weight * x - robin_s[...]
        sent = pick_lanes(outgoing, slots_s[...])
        for s in range(slots_s.shape[1] // LANES):
            robin_send[t, s] = sent[:, s * LANES : (s + 1) * LANES]
        for off in range(1, peers):
            robin_copy(t, off).start()
        bx = apply(x)
        base = lax.rem(me * cap, LANES)
        inside = inside_s[...] + base
        owner = owner_s[...]
        fresh = jnp.zeros((rows, faces), jnp.float32)
        for off in range(1, peers):
            robin_copy(t, off).wait_recv()
            source = lax.rem(me + peers - off, peers)
            got = pick_lanes(robin_recv[t, off - 1], inside)
            fresh = jnp.where(owner == source, got, fresh)
        robin_s[...] = fresh
        trace_s[...] = sweep(x, bx)
        pl.when(t < ITERS - 1)(front)
        for r in range(CSWEEPS):
            wait_rows(t, r, coarse_send_sem)
        for off in range(1, peers):
            robin_copy(t, off).wait_send()
        return carry

    lax.fori_loop(0, ITERS, iteration, 0)
    for a in range(trace_dim):
        trace_out[0, a] = kept_s[a : a + 1, :]
        robin_out[0, a] = robin_s[a : a + 1, :]


def hand_out(*refs):
    sems = refs[-1]
    count = len(refs) // 2
    copies = [pltpu.make_async_copy(refs[i], refs[count + i], sems.at[i]) for i in range(count)]
    for copy in copies:
        copy.start()
    for copy in copies:
        copy.wait()


def solution(mesh):
    groups, peers = mesh.shape["grp"], mesh.shape["sub"]

    def body(
        load,
        couple,
        face_link,
        face_count,
        slot_face,
        pair_count,
        basis,
        coarse_inverse,
        coarse_block,
        coarse_link,
    ):
        trace_dim, faces = load.shape[-2:]
        rows = -(-trace_dim // 8) * 8
        links = face_link.shape[-2]
        cvec = basis.shape[2]
        kc = coarse_link.shape[-1]
        cap = slot_face.shape[-1]
        chunks = -(-peers * cap // LANES)
        vmem, smem = pltpu.VMEM, pltpu.SMEM
        operands = (
            jnp.swapaxes(load, 1, 2),
            jnp.transpose(couple, (0, 1, 3, 4, 2, 5)),
            jnp.swapaxes(face_link, 1, 2),
            face_count,
            slot_face,
            pair_count,
            jnp.swapaxes(basis, 2, 3),
            coarse_inverse,
            coarse_block,
            coarse_link,
        )
        f32 = jnp.float32
        spec = lambda space: pl.BlockSpec(memory_space=space)
        results = pl.pallas_call(
            functools.partial(kernel, groups, peers),
            out_shape=(
                jax.ShapeDtypeStruct((1, trace_dim, 1, faces), f32),
                jax.ShapeDtypeStruct((1, trace_dim, 1, faces), f32),
                jax.ShapeDtypeStruct((1, 1, cvec), f32),
            ),
            in_specs=[spec(pltpu.HBM)] * len(operands),
            out_specs=(spec(vmem), spec(vmem), spec(vmem)),
            scratch_shapes=[
                space(x.shape, x.dtype)
                for x, space in zip(operands, (vmem, vmem, vmem, smem, vmem, smem, vmem, vmem, vmem, smem))
            ]
            + [
                vmem((rows, faces), f32),
                vmem((rows, faces), f32),
                vmem((rows, faces), f32),
                vmem((links + 1, rows, faces), f32),
                vmem((faces // LANES, trace_dim, (links + 1) * rows, LANES), f32),
                vmem((rows, faces), f32),
                vmem((rows, faces), f32),
                vmem((3 * peers, 1, LANES), f32),
                vmem((kc, cvec, cvec), f32),
                vmem((1, chunks * LANES), jnp.int32),
                vmem((1, faces), jnp.int32),
                vmem((1, faces), jnp.int32),
                vmem((1, faces), f32),
                vmem((cvec, LANES), f32),
                vmem((ITERS, CSWEEPS, 1, LANES), f32),
                vmem((ITERS, CSWEEPS, 3 * peers, 1, LANES), f32),
                vmem((ITERS, chunks, rows, LANES), f32),
                vmem((ITERS, peers - 1, rows, LANES), f32),
                pltpu.SemaphoreType.DMA((ITERS, CSWEEPS, 3)),
                pltpu.SemaphoreType.DMA((ITERS, CSWEEPS, 3)),
                pltpu.SemaphoreType.DMA((ITERS, peers - 1)),
                pltpu.SemaphoreType.DMA((ITERS, peers - 1)),
                pltpu.SemaphoreType.DMA((len(operands),)),
            ],
            compiler_params=pltpu.CompilerParams(
                collective_id=0, has_side_effects=True, vmem_limit_bytes=24 * 1024 * 1024
            ),
        )(*operands)
        trace_field, robin_data, coefficients = pl.pallas_call(
            hand_out,
            out_shape=tuple(jax.ShapeDtypeStruct(x.shape, x.dtype) for x in results),
            in_specs=[spec(vmem)] * 3,
            out_specs=(spec(pl.ANY),) * 3,
            scratch_shapes=[pltpu.SemaphoreType.DMA((3,))],
        )(*results)
        return jnp.swapaxes(trace_field, 1, 2), jnp.swapaxes(robin_data, 1, 2), coefficients

    in_specs = (
        P("grp", "sub", None, None),
        P("grp", "sub", None, None, None, None),
        P("grp", "sub", None, None),
        P("grp", "sub"),
        P("grp", "sub", None, None),
        P("grp", "sub", None),
        P("grp", "sub", None, None, None),
        P("grp", "sub", None, None),
        P("grp", "sub", None, None, None),
        P("grp", "sub", None),
    )
    out_specs = (P("grp", "sub", None, None), P("grp", "sub", None, None), P("grp", "sub", None))
    return jax.shard_map(body, mesh=mesh, in_specs=in_specs, out_specs=out_specs, check_vma=False)
```

profile of v0, /device:TPU:0, one launch (start us, length us, event | category | flops | bytes accessed | tf_op | source)
XLA Modules:
  0.0 49.8 jit_solution(17591828146422919944)
XLA Ops:
  1.3 0.0 copy-start
  1.3 1.4 %copy-done = f32[1,1,64,15,384]{4,2,3,1,0:T(8,128)S(1)} copy-done((f32[1,1,64,15,384]{4,2,3,1,0:T(8,128)S(1)}, f32[1,1,64,15,384]{4,2,3,1,0:T(8,128)}, u32[]{:S(2)}) %copy-start) | copy-done | bytes 1474584
  2.7 0.0 copy-start.1
  2.7 1.1 %copy-done.1 = bf16[1,1,4,15,15,384]{5,2,4,3,1,0:T(4,128)(2,1)S(1)} copy-done((bf16[1,1,4,15,15,384]{5,2,4,3,1,0:T(4,128)(2,1)S(1)}, bf16[1,1,4,15,15,384]{5,2,4,3,1,0:T(4,128)(2,1)}, u32[]{:S(2)}) %copy-start.1) | copy-done | bytes 691224
  3.8 0.0 copy-start.2
  3.8 0.9 %copy-done.2 = f32[1,1,6,64,64]{4,3,2,1,0:T(8,128)S(1)} copy-done((f32[1,1,6,64,64]{4,3,2,1,0:T(8,128)S(1)}, f32[1,1,6,64,64]{4,3,2,1,0:T(8,128)}, u32[]{:S(2)}) %copy-start.2) | copy-done | bytes 98328
  4.7 0.0 copy-start.3
  4.7 0.8 %copy-done.3 = f32[1,1,64,64]{3,2,1,0:T(8,128)S(1)} copy-done((f32[1,1,64,64]{3,2,1,0:T(8,128)S(1)}, f32[1,1,64,64]{3,2,1,0:T(8,128)}, u32[]{:S(2)}) %copy-start.3) | copy-done | bytes 16408
  5.4 0.0 copy-start.4
  5.4 0.7 %copy-done.4 = f32[1,1,15,384]{3,1,2,0:T(1,128)S(1)} copy-done((f32[1,1,15,384]{3,1,2,0:T(1,128)S(1)}, f32[1,1,15,384]{3,1,2,0:T(1,128)}, u32[]{:S(2)}) %copy-start.4) | copy-done | bytes 23064
  6.2 0.0 copy-start.7
  6.2 0.7 %copy-done.7 = s32[1,1,3,384]{3,1,2,0:T(1,128)S(1)} copy-done((s32[1,1,3,384]{3,1,2,0:T(1,128)S(1)}, s32[1,1,3,384]{3,1,2,0:T(1,128)}, u32[]{:S(2)}) %copy-start.7) | copy-done | bytes 4632
  6.9 0.0 copy-start.8
  6.9 0.7 %copy-done.8 = s32[1,1,4,32]{3,2,1,0:T(4,128)S(1)} copy-done((s32[1,1,4,32]{3,2,1,0:T(4,128)S(1)}, s32[1,1,4,32]{3,2,1,0:T(4,128)}, u32[]{:S(2)}) %copy-start.8) | copy-done | bytes 536
  7.5 0.0 copy-start.9
  7.5 0.7 %copy-done.9 = s32[1,1,4]{2,1,0:T(1,128)S(1)} copy-done((s32[1,1,4]{2,1,0:T(1,128)S(1)}, s32[1,1,4]{2,1,0:T(1,128)}, u32[]{:S(2)}) %copy-start.9) | copy-done | bytes 40
  8.2 0.0 copy-start.10
  8.2 0.7 %copy-done.10 = s32[1,1,6]{2,1,0:T(1,128)S(1)} copy-done((s32[1,1,6]{2,1,0:T(1,128)S(1)}, s32[1,1,6]{2,1,0:T(1,128)}, u32[]{:S(2)}) %copy-start.10) | copy-done | bytes 48
  8.9 37.8 %shard_map.121 = (f32[1,15,1,384]{3,2,1,0:T(1,128)S(1)}, f32[1,15,1,384]{3,2,1,0:T(1,128)S(1)}, f32[1,1,64]{2,1,0:T(1,128)S(1)}) custom-call(f32[1,15,1,384]{3,2,1,0:T(1,128)S(1)} %bitcast.12, bf16[1,1,15,15,4,384]{5,4,3,2,1,0:T(4,128)(2,1)S(1)} %bitcast.11, s32[1,3,1,384]{3,2,1,0:T(1,128)S(1)} %bitcast.13, s32[1,1]{1,0:T(1,128)S(6)} %copy.15.count_hbm, ...), custom_call_target="tpu_custom_call" | custom-call | tf_op jit(solution)/shard_map/pallas_call | solution.py:380
  46.7 0.0 copy-start.5
  46.7 0.6 %copy-done.5 = f32[1,15,1,384]{3,2,1,0:T(1,128)} copy-done((f32[1,15,1,384]{3,2,1,0:T(1,128)}, f32[1,15,1,384]{3,2,1,0:T(1,128)S(1)}, u32[]{:S(2)}) %copy-start.5) | copy-done | bytes 23064
  47.3 0.0 copy-start.6
  47.3 0.6 %copy-done.6 = f32[1,15,1,384]{3,2,1,0:T(1,128)} copy-done((f32[1,15,1,384]{3,2,1,0:T(1,128)}, f32[1,15,1,384]{3,2,1,0:T(1,128)S(1)}, u32[]{:S(2)}) %copy-start.6) | copy-done | bytes 23064
  47.9 0.0 copy-start.11
  47.9 0.5 copy-done.11
  48.4 1.4 %shard_map.122 = (f32[1,15,1,384]{3,2,1,0:T(1,128)}, f32[1,15,1,384]{3,2,1,0:T(1,128)}, f32[1,1,64]{2,1,0:T(1,128)}) custom-call(f32[1,15,1,384]{3,2,1,0:T(1,128)} %copy-done.5, f32[1,15,1,384]{3,2,1,0:T(1,128)} %copy-done.6, f32[1,1,64]{2,1,0:T(1,128)} %copy-done.11), custom_call_target="tpu_custom_call" | custom-call | tf_op jit(solution)/shard_map/pallas_call | solution.py:422
Async XLA Ops:
  1.3 1.4 %copy-start = (f32[1,1,64,15,384]{4,2,3,1,0:T(8,128)S(1)}, f32[1,1,64,15,384]{4,2,3,1,0:T(8,128)}, u32[]{:S(2)}) copy-start(f32[1,1,64,15,384]{4,2,3,1,0:T(8,128)} %param.16) | copy-start | bytes 4423684
  2.7 1.1 %copy-start.1 = (bf16[1,1,4,15,15,384]{5,2,4,3,1,0:T(4,128)(2,1)S(1)}, bf16[1,1,4,15,15,384]{5,2,4,3,1,0:T(4,128)(2,1)}, u32[]{:S(2)}) copy-start(bf16[1,1,4,15,15,384]{5,2,4,3,1,0:T(4,128)(2,1)} %param.11) | copy-start | bytes 2073604
  3.8 0.9 %copy-start.2 = (f32[1,1,6,64,64]{4,3,2,1,0:T(8,128)S(1)}, f32[1,1,6,64,64]{4,3,2,1,0:T(8,128)}, u32[]{:S(2)}) copy-start(f32[1,1,6,64,64]{4,3,2,1,0:T(8,128)} %block_hbm.1) | copy-start | bytes 294916
  4.7 0.8 %copy-start.3 = (f32[1,1,64,64]{3,2,1,0:T(8,128)S(1)}, f32[1,1,64,64]{3,2,1,0:T(8,128)}, u32[]{:S(2)}) copy-start(f32[1,1,64,64]{3,2,1,0:T(8,128)} %inverse_hbm.1) | copy-start | bytes 49156
  5.4 0.7 %copy-start.4 = (f32[1,1,15,384]{3,1,2,0:T(1,128)S(1)}, f32[1,1,15,384]{3,1,2,0:T(1,128)}, u32[]{:S(2)}) copy-start(f32[1,1,15,384]{3,1,2,0:T(1,128)} %param.10) | copy-start | bytes 69124
  6.2 0.7 %copy-start.7 = (s32[1,1,3,384]{3,1,2,0:T(1,128)S(1)}, s32[1,1,3,384]{3,1,2,0:T(1,128)}, u32[]{:S(2)}) copy-start(s32[1,1,3,384]{3,1,2,0:T(1,128)} %param.12) | copy-start | bytes 13828
  6.9 0.7 %copy-start.8 = (s32[1,1,4,32]{3,2,1,0:T(4,128)S(1)}, s32[1,1,4,32]{3,2,1,0:T(4,128)}, u32[]{:S(2)}) copy-start(s32[1,1,4,32]{3,2,1,0:T(4,128)} %slot_hbm.1) | copy-start | bytes 1540
  7.5 0.7 %copy-start.9 = (s32[1,1,4]{2,1,0:T(1,128)S(1)}, s32[1,1,4]{2,1,0:T(1,128)}, u32[]{:S(2)}) copy-start(s32[1,1,4]{2,1,0:T(1,128)} %pair_hbm.1) | copy-start | bytes 52
  8.2 0.7 %copy-start.10 = (s32[1,1,6]{2,1,0:T(1,128)S(1)}, s32[1,1,6]{2,1,0:T(1,128)}, u32[]{:S(2)}) copy-start(s32[1,1,6]{2,1,0:T(1,128)} %coarse_link_hbm.1) | copy-start | bytes 76
  46.7 0.6 %copy-start.5 = (f32[1,15,1,384]{3,2,1,0:T(1,128)}, f32[1,15,1,384]{3,2,1,0:T(1,128)S(1)}, u32[]{:S(2)}) copy-start(f32[1,15,1,384]{3,2,1,0:T(1,128)S(1)} %get-tuple-element.9.refs_0_) | copy-start | bytes 69124
  47.3 0.6 %copy-start.6 = (f32[1,15,1,384]{3,2,1,0:T(1,128)}, f32[1,15,1,384]{3,2,1,0:T(1,128)S(1)}, u32[]{:S(2)}) copy-start(f32[1,15,1,384]{3,2,1,0:T(1,128)S(1)} %get-tuple-element.10.refs_1_) | copy-start | bytes 69124
  47.9 0.5 copy-start.11
where the time goes:
time: 50.3 us; the launch traced here: 49.8 us
  Pallas kernels  39.2 us (78%)
  local copies, waits for them, and re-layouts  9.23 us (18%)
  between operations  1.31 us (3%)
    pallas_call x1, Pallas kernels, body(): pl.pallas_call(functools.partial(kernel, groups, peers), out_shape=(jax.S...  37.8 us
    unnamed x24, local copies, waits for them, and re-layouts  9.23 us
    pallas_call x1, Pallas kernels, body(): pl.pallas_call(hand_out, out_shape=tuple((jax.ShapeDtypeStruct(x.shape, x...  1.39 us

commit v1 on v0

--- a/solution.py
+++ b/solution.py
@@ -79,6 +79,7 @@
     owner_s,
     interface_s,
     start_s,
+    coef_s,
     coarse_send,
     coarse_recv,
     robin_send,
@@ -109,9 +110,12 @@
 
         act(0)
 
+    def after(off):
+        return jnp.where(me + off >= peers, me + off - peers, me + off)
+
     def targets(d):
         first = 1 if d == 0 else 0
-        return [(g + d, lax.rem(me + off, peers)) for off in range(first, peers)]
+        return [(g + d, after(off)) for off in range(first, peers)]
 
     operands = (
         (count_hbm, count_ref),
@@ -181,6 +185,8 @@
 
     fetches[5].wait()
     lax.fori_loop(0, trace_dim, unpack, 0)
+    count = (peers - 1) + jnp.where(g > 0, peers, 0) + jnp.where(g < groups - 1, peers, 0)
+
     def apply(x):
         stack_s[0] = x
         for k in range(links):
@@ -243,7 +249,7 @@
         return jnp.sum(total, axis=1, keepdims=True)
 
     def robin_copy(t, off):
-        to = lax.rem(me + off, peers)
+        to = after(off)
         chunk = lax.div(to * cap, LANES)
         return pltpu.make_async_remote_copy(
             src_ref=robin_send.at[t, chunk],
@@ -254,12 +260,20 @@
             device_id_type=MESH,
         )
 
-    def front():
-        x = trace_s[...]
-        for _ in range(SWEEPS - 1):
-            x = sweep(x, apply(x))
-        residual = right_side() - apply(x)
-        trace_s[...] = x
+    def fold():
+        for k in range(kc):
+            folded_s[k] = jnp.dot(
+                inverse_ref[0, 0],
+                block_ref[0, 0, k],
+                precision=highest,
+                preferred_element_type=jnp.float32,
+            )
+
+    def relax(bx):
+        trace_s[...] = sweep(trace_s[...], bx)
+
+    def coarse(t, bx):
+        residual = right_side() - bx
         part = jnp.zeros((cvec, LANES), jnp.float32)
         for a in range(trace_dim):
             product = basis_ref[0, 0, a] * residual[a : a + 1, :]
@@ -268,36 +282,22 @@
         restricted = jnp.sum(part, axis=1, keepdims=True)
         start = jnp.sum(inverse_ref[0, 0] * as_row(restricted), axis=1, keepdims=True)
         start_s[...] = jnp.broadcast_to(start, start_s.shape)
-
-    def fold():
-        for k in range(kc):
-            folded_s[k] = jnp.dot(
-                inverse_ref[0, 0],
-                block_ref[0, 0, k],
-                precision=highest,
-                preferred_element_type=jnp.float32,
-            )
-
-    for fetch in fetches[6:]:
-        fetch.wait()
-    front()
-    count = (peers - 1) + jnp.where(g > 0, peers, 0) + jnp.where(g < groups - 1, peers, 0)
-    pl.semaphore_wait(barrier, count)
-
-    def iteration(t, carry):
-        start = start_s[:, 0:1]
-        coef = start
-        for r in range(CSWEEPS):
-            send_row(t, r, as_row(coef))
-            if r == 0:
-                pl.when(t == 0)(fold)
+        coef_s[...] = start_s[...]
+
+        def exchange(r, carry):
+            send_row(t, r, as_row(coef_s[:, 0:cvec]))
+            pl.when((t == 0) & (r == 0))(fold)
             wait_rows(t, r, coarse_recv_sem)
-            coef = start - coupled(t, r)
-        coef_out[0] = as_row(coef)
-        wide = jnp.broadcast_to(coef, (cvec, faces))
+            coef_s[...] = start_s[...] - coupled(t, r)
+            return carry
+
+        lax.fori_loop(0, CSWEEPS, exchange, 0)
+        coef_out[0] = as_row(coef_s[:, 0:cvec])
+        wide = jnp.concatenate([coef_s[...]] * (faces // LANES), axis=1)
         for a in range(trace_dim):
             moved_s[a : a + 1, :] = jnp.sum(basis_ref[0, 0, a] * wide, axis=0, keepdims=True)
         x = trace_s[...] + live * moved_s[...]
+        trace_s[...] = x
         kept_s[...] = x
         outgoing = 2.0 * robin_weight * x - robin_s[...]
         sent = pick_lanes(outgoing, slots_s[...])
@@ -305,39 +305,46 @@
             robin_send[t, s] = sent[:, s * LANES : (s + 1) * LANES]
         for off in range(1, peers):
             robin_copy(t, off).start()
-        bx = apply(x)
+
+    def settle(t, bx):
         base = lax.rem(me * cap, LANES)
         inside = inside_s[...] + base
         owner = owner_s[...]
         fresh = jnp.zeros((rows, faces), jnp.float32)
         for off in range(1, peers):
             robin_copy(t, off).wait_recv()
-            source = lax.rem(me + peers - off, peers)
+            source = after(peers - off)
             got = pick_lanes(robin_recv[t, off - 1], inside)
             fresh = jnp.where(owner == source, got, fresh)
         robin_s[...] = fresh
-        trace_s[...] = sweep(x, bx)
-        pl.when(t < ITERS - 1)(front)
+        trace_s[...] = sweep(trace_s[...], bx)
         for r in range(CSWEEPS):
             wait_rows(t, r, coarse_send_sem)
         for off in range(1, peers):
             robin_copy(t, off).wait_send()
+
+    phases = SWEEPS + 1
+
+    def step(n, carry):
+        t = n // phases
+        phase = n - t * phases
+        bx = apply(trace_s[...])
+        pl.when(phase < SWEEPS - 1)(lambda: relax(bx))
+
+        @pl.when(n == SWEEPS - 1)
+        def _():
+            pl.semaphore_wait(barrier, count)
+            for fetch in fetches[6:]:
+                fetch.wait()
+
+        pl.when(phase == SWEEPS - 1)(lambda: coarse(t, bx))
+        pl.when(phase == SWEEPS)(lambda: settle(t, bx))
         return carry
 
-    lax.fori_loop(0, ITERS, iteration, 0)
+    lax.fori_loop(0, ITERS * phases, step, 0)
     for a in range(trace_dim):
         trace_out[0, a] = kept_s[a : a + 1, :]
         robin_out[0, a] = robin_s[a : a + 1, :]
-
-
-def hand_out(*refs):
-    sems = refs[-1]
-    count = len(refs) // 2
-    copies = [pltpu.make_async_copy(refs[i], refs[count + i], sems.at[i]) for i in range(count)]
-    for copy in copies:
-        copy.start()
-    for copy in copies:
-        copy.wait()
 
 
 def solution(mesh):
@@ -377,7 +384,7 @@
         )
         f32 = jnp.float32
         spec = lambda space: pl.BlockSpec(memory_space=space)
-        results = pl.pallas_call(
+        trace_field, robin_data, coefficients = pl.pallas_call(
             functools.partial(kernel, groups, peers),
             out_shape=(
                 jax.ShapeDtypeStruct((1, trace_dim, 1, faces), f32),
@@ -405,6 +412,7 @@
                 vmem((1, faces), jnp.int32),
                 vmem((1, faces), f32),
                 vmem((cvec, LANES), f32),
+                vmem((cvec, LANES), f32),
                 vmem((ITERS, CSWEEPS, 1, LANES), f32),
                 vmem((ITERS, CSWEEPS, 3 * peers, 1, LANES), f32),
                 vmem((ITERS, chunks, rows, LANES), f32),
@@ -416,16 +424,9 @@
                 pltpu.SemaphoreType.DMA((len(operands),)),
             ],
             compiler_params=pltpu.CompilerParams(
-                collective_id=0, has_side_effects=True, vmem_limit_bytes=24 * 1024 * 1024
+                collective_id=0, has_side_effects=True, vmem_limit_bytes=56 * 1024 * 1024
             ),
         )(*operands)
-        trace_field, robin_data, coefficients = pl.pallas_call(
-            hand_out,
-            out_shape=tuple(jax.ShapeDtypeStruct(x.shape, x.dtype) for x in results),
-            in_specs=[spec(vmem)] * 3,
-            out_specs=(spec(pl.ANY),) * 3,
-            scratch_shapes=[pltpu.SemaphoreType.DMA((3,))],
-        )(*results)
         return jnp.swapaxes(trace_field, 1, 2), jnp.swapaxes(robin_data, 1, 2), coefficients
 
     in_specs = (

time: 50.3 us -> 43.3 us (0.86)
  local copies, waits for them, and re-layouts: 9.23 us -> 3.82 us
  Pallas kernels: 39.2 us -> 37.9 us
    unnamed x24 -> x3, local copies, waits for them, and re-layouts: 9.23 us -> 3.82 us
    pallas_call x1 -> x0, Pallas kernels: 1.39 us -> none  [body(): pl.pallas_call(hand_out, out_shape=tuple((jax.ShapeDtypeStruct(x.shape, x...]
where the time goes in v1:
time: 43.3 us; the launch traced here: 43 us
  Pallas kernels  37.9 us (88%)
  local copies, waits for them, and re-layouts  3.82 us (9%)
  between operations  1.29 us (3%)
    pallas_call x1, Pallas kernels, body(): pl.pallas_call(functools.partial(kernel, groups, peers), out_shape=(jax.S...  37.9 us
    unnamed x3, local copies, waits for them, and re-layouts  3.82 us

profile of v1, /device:TPU:0, one launch (start us, length us, event | category | flops | bytes accessed | tf_op | source)
XLA Modules:
  0.0 43.0 jit_solution(17064663004467740518)
XLA Ops:
  1.3 37.9 %shard_map.121 = (f32[1,15,1,384]{3,2,1,0:T(1,128)}, f32[1,15,1,384]{3,2,1,0:T(1,128)}, f32[1,1,64]{2,1,0:T(1,128)}) custom-call(f32[1,15,1,384]{3,2,1,0:T(1,128)} %bitcast.12, bf16[1,1,15,15,4,384]{5,4,3,2,1,0:T(4,128)(2,1)} %bitcast.11, s32[1,3,1,384]{3,2,1,0:T(1,128)} %bitcast.15, s32[1,1]{1,0:T(1,128)S(6)} %copy.18.count_hbm, s32[1,1,4,32]{3,2,1,0:T(4,128)} %slot_hbm.1, ...), custom_call_target="tpu_custom_call" | custom-call | tf_op jit(solution)/shard_map/pallas_call | solution.py:387
  39.2 1.4 %copy.19 = f32[1,1,15,384]{3,1,2,0:T(1,128)} copy(f32[1,1,15,384]{3,1,2,0:T(1,128)} %bitcast.14) | data formatting | bytes 46080
  40.5 1.4 %copy.20 = f32[1,1,15,384]{3,1,2,0:T(1,128)} copy(f32[1,1,15,384]{3,1,2,0:T(1,128)} %bitcast.13) | data formatting | bytes 46080
  41.9 1.1 %copy.21 = f32[1,1,64]{2,1,0:T(1,128)} copy(f32[1,1,64]{2,1,0:T(1,128)} %get-tuple-element.17) | data formatting | bytes 512

commit v2 on v1

--- a/solution.py
+++ b/solution.py
@@ -18,21 +18,19 @@
 MESH = pl.DeviceIdType.MESH
 
 
-def pick_lanes(field, index):
+def pick_lanes(field, hot):
+    pieces, rest = [], field
+    for _ in range(3):
+        piece = rest.astype(jnp.bfloat16)
+        rest = rest - piece.astype(jnp.float32)
+        pieces.append(piece)
+    got = jnp.dot(jnp.concatenate(pieces, axis=0), hot, preferred_element_type=jnp.float32)
     rows = field.shape[0]
-    parts = []
-    for d in range(index.shape[1] // LANES):
-        wanted = jnp.broadcast_to(index[:, d * LANES : (d + 1) * LANES], (rows, LANES))
-        within = wanted & (LANES - 1)
-        chunk = wanted >> (LANES.bit_length() - 1)
-        out = None
-        for s in range(field.shape[1] // LANES):
-            got = jnp.take_along_axis(
-                field[:, s * LANES : (s + 1) * LANES], within, axis=1, mode="promise_in_bounds"
-            )
-            out = got if out is None else jnp.where(chunk == s, got, out)
-        parts.append(out)
-    return jnp.concatenate(parts, axis=1) if len(parts) > 1 else parts[0]
+    return got[0:rows] + got[rows : 2 * rows] + got[2 * rows : 3 * rows]
+
+
+def one_hot(index, count):
+    return jnp.where(iota((count, index.shape[1]), 0) == index, 1.0, 0.0).astype(jnp.bfloat16)
 
 
 def iota(shape, dim):
@@ -75,8 +73,9 @@
     table_s,
     folded_s,
     slots_s,
-    inside_s,
-    owner_s,
+    link_hot,
+    out_hot,
+    in_hot,
     interface_s,
     start_s,
     coef_s,
@@ -177,8 +176,15 @@
         inside = jnp.where(found >= 0.0, found, inside)
         owner = jnp.where(found >= 0.0, float(j), owner)
     interface_s[...] = jnp.where(owner >= 0.0, 1.0, 0.0)
-    inside_s[...] = inside.astype(jnp.int32)
-    owner_s[...] = owner.astype(jnp.int32)
+    owner = owner.astype(jnp.int32)
+    base = lax.rem(me * cap, LANES)
+    for off in range(1, peers):
+        rows_at = slice((off - 1) * LANES, off * LANES)
+        wanted = jnp.where(owner == after(peers - off), inside.astype(jnp.int32) + base, -1)
+        in_hot[rows_at, :] = one_hot(wanted, LANES)
+    out_hot[...] = one_hot(slots_s[...], faces)
+    for k in range(links):
+        link_hot[:, k * faces : (k + 1) * faces] = one_hot(link_ref[0, k], faces)
     robin_s[...] = jnp.zeros_like(robin_s)
     trace_s[...] = omega_step * load_s[...]
     eye = iota((cvec, cvec), 0) == iota((cvec, cvec), 1)
@@ -189,8 +195,9 @@
 
     def apply(x):
         stack_s[0] = x
+        linked = pick_lanes(x, link_hot[...])
         for k in range(links):
-            stack_s[k + 1] = pick_lanes(x, link_ref[0, k])
+            stack_s[k + 1] = linked[:, k * faces : (k + 1) * faces]
         chunks = []
         for s in range(faces // LANES):
             lanes = slice(s * LANES, (s + 1) * LANES)
@@ -300,22 +307,17 @@
         trace_s[...] = x
         kept_s[...] = x
         outgoing = 2.0 * robin_weight * x - robin_s[...]
-        sent = pick_lanes(outgoing, slots_s[...])
+        sent = pick_lanes(outgoing, out_hot[...])
         for s in range(slots_s.shape[1] // LANES):
             robin_send[t, s] = sent[:, s * LANES : (s + 1) * LANES]
         for off in range(1, peers):
             robin_copy(t, off).start()
 
     def settle(t, bx):
-        base = lax.rem(me * cap, LANES)
-        inside = inside_s[...] + base
-        owner = owner_s[...]
-        fresh = jnp.zeros((rows, faces), jnp.float32)
         for off in range(1, peers):
             robin_copy(t, off).wait_recv()
-            source = after(peers - off)
-            got = pick_lanes(robin_recv[t, off - 1], inside)
-            fresh = jnp.where(owner == source, got, fresh)
+        arrived = jnp.concatenate([robin_recv[t, off - 1] for off in range(1, peers)], axis=1)
+        fresh = pick_lanes(arrived, in_hot[...])
         robin_s[...] = fresh
         trace_s[...] = sweep(trace_s[...], bx)
         for r in range(CSWEEPS):
@@ -391,7 +393,7 @@
                 jax.ShapeDtypeStruct((1, trace_dim, 1, faces), f32),
                 jax.ShapeDtypeStruct((1, 1, cvec), f32),
             ),
-            in_specs=[spec(pltpu.HBM)] * len(operands),
+            in_specs=[spec(pl.ANY)] * len(operands),
             out_specs=(spec(vmem), spec(vmem), spec(vmem)),
             scratch_shapes=[
                 space(x.shape, x.dtype)
@@ -408,8 +410,9 @@
                 vmem((3 * peers, 1, LANES), f32),
                 vmem((kc, cvec, cvec), f32),
                 vmem((1, chunks * LANES), jnp.int32),
-                vmem((1, faces), jnp.int32),
-                vmem((1, faces), jnp.int32),
+                vmem((faces, links * faces), jnp.bfloat16),
+                vmem((faces, chunks * LANES), jnp.bfloat16),
+                vmem(((peers - 1) * LANES, faces), jnp.bfloat16),
                 vmem((1, faces), f32),
                 vmem((cvec, LANES), f32),
                 vmem((cvec, LANES), f32),
@@ -424,9 +427,9 @@
                 pltpu.SemaphoreType.DMA((len(operands),)),
             ],
             compiler_params=pltpu.CompilerParams(
-                collective_id=0, has_side_effects=True, vmem_limit_bytes=56 * 1024 * 1024
+                collective_id=0, has_side_effects=True, vmem_limit_bytes=24 * 1024 * 1024
             ),
-        )(*operands)
+        )(*(x if x.size == 1 else pltpu.with_memory_space_constraint(x, pltpu.HBM) for x in operands))
         return jnp.swapaxes(trace_field, 1, 2), jnp.swapaxes(robin_data, 1, 2), coefficients
 
     in_specs = (

time: 43.3 us -> 41.7 us (0.963)
  local copies, waits for them, and re-layouts: 3.82 us -> 1.73 us
  Pallas kernels: 37.9 us -> 38.5 us
    unnamed x3, local copies, waits for them, and re-layouts: 3.82 us -> 1.73 us
    pallas_call x1, Pallas kernels: 37.9 us -> 38.5 us  [body(): pl.pallas_call(functools.partial(kernel, groups, peers), out_shape=(jax.S...]
where the time goes in v2:
time: 41.7 us; the launch traced here: 41.5 us
  Pallas kernels  38.5 us (92%)
  local copies, waits for them, and re-layouts  1.73 us (4%)
  between operations  1.29 us (3%)
    pallas_call x1, Pallas kernels, body(): pl.pallas_call(functools.partial(kernel, groups, peers), out_shape=(jax.S...  38.5 us
    unnamed x3, local copies, waits for them, and re-layouts  1.73 us

profile of v2, /device:TPU:0, one launch (start us, length us, event | category | flops | bytes accessed | tf_op | source)
XLA Modules:
  0.0 41.5 jit_solution(5596710592547565551)
XLA Ops:
  1.3 38.5 %shard_map.121 = (f32[1,15,1,384]{3,2,1,0:T(1,128)S(1)}, f32[1,15,1,384]{3,2,1,0:T(1,128)S(1)}, f32[1,1,64]{2,1,0:T(1,128)S(1)}) custom-call(f32[1,15,1,384]{3,2,1,0:T(1,128)} %bitcast.14, bf16[1,1,15,15,4,384]{5,4,3,2,1,0:T(4,128)(2,1)} %bitcast.13, s32[1,3,1,384]{3,2,1,0:T(1,128)} %bitcast.15, s32[1,1]{1,0:T(1,128)S(6)} %copy.18.count_hbm, ...), custom_call_target="tpu_custom_call" | custom-call | tf_op jit(solution)/shard_map/pallas_call | solution.py:389
  39.8 0.6 %copy.19 = f32[1,1,15,384]{3,1,2,0:T(1,128)} copy(f32[1,1,15,384]{3,1,2,0:T(1,128)S(1)} %bitcast.11) | data formatting | bytes 46080
  40.4 0.6 %copy.20 = f32[1,1,15,384]{3,1,2,0:T(1,128)} copy(f32[1,1,15,384]{3,1,2,0:T(1,128)S(1)} %bitcast.10) | data formatting | bytes 46080
  41.0 0.5 %copy.21 = f32[1,1,64]{2,1,0:T(1,128)} copy(f32[1,1,64]{2,1,0:T(1,128)S(1)} %get-tuple-element.17) | data formatting | bytes 512

commit v3 on v1

--- a/solution.py
+++ b/solution.py
@@ -71,7 +71,6 @@
     stack_s,
     couple_s,
     moved_s,
-    kept_s,
     table_s,
     folded_s,
     slots_s,
@@ -115,7 +114,15 @@
 
     def targets(d):
         first = 1 if d == 0 else 0
-        return [(g + d, after(off)) for off in range(first, peers)]
+        offsets = sorted(range(first, peers), key=lambda off: -min(off, peers - off))
+        return [(g + d, after(off)) for off in offsets]
+
+    def far_first(act):
+        even = lax.rem(g, 2) == 0
+        pl.when(even & (g > 0))(lambda: act(-1))
+        pl.when(g < groups - 1)(lambda: act(1))
+        pl.when(jnp.logical_not(even))(lambda: act(-1))
+        act(0)
 
     operands = (
         (count_hbm, count_ref),
@@ -228,7 +235,7 @@
                     device_id_type=MESH,
                 ).start()
 
-        per_group(push)
+        far_first(push)
 
     def wait_rows(t, r, sems):
         def wait(d):
@@ -298,13 +305,14 @@
             moved_s[a : a + 1, :] = jnp.sum(basis_ref[0, 0, a] * wide, axis=0, keepdims=True)
         x = trace_s[...] + live * moved_s[...]
         trace_s[...] = x
-        kept_s[...] = x
         outgoing = 2.0 * robin_weight * x - robin_s[...]
         sent = pick_lanes(outgoing, slots_s[...])
         for s in range(slots_s.shape[1] // LANES):
             robin_send[t, s] = sent[:, s * LANES : (s + 1) * LANES]
         for off in range(1, peers):
             robin_copy(t, off).start()
+        for a in range(trace_dim):
+            trace_out[0, a] = x[a : a + 1, :]
 
     def settle(t, bx):
         base = lax.rem(me * cap, LANES)
@@ -343,7 +351,6 @@
 
     lax.fori_loop(0, ITERS * phases, step, 0)
     for a in range(trace_dim):
-        trace_out[0, a] = kept_s[a : a + 1, :]
         robin_out[0, a] = robin_s[a : a + 1, :]
 
 
@@ -391,7 +398,7 @@
                 jax.ShapeDtypeStruct((1, trace_dim, 1, faces), f32),
                 jax.ShapeDtypeStruct((1, 1, cvec), f32),
             ),
-            in_specs=[spec(pltpu.HBM)] * len(operands),
+            in_specs=[spec(pl.ANY)] * len(operands),
             out_specs=(spec(vmem), spec(vmem), spec(vmem)),
             scratch_shapes=[
                 space(x.shape, x.dtype)
@@ -403,7 +410,6 @@
                 vmem((rows, faces), f32),
                 vmem((links + 1, rows, faces), f32),
                 vmem((faces // LANES, trace_dim, (links + 1) * rows, LANES), f32),
-                vmem((rows, faces), f32),
                 vmem((rows, faces), f32),
                 vmem((3 * peers, 1, LANES), f32),
                 vmem((kc, cvec, cvec), f32),
@@ -424,9 +430,9 @@
                 pltpu.SemaphoreType.DMA((len(operands),)),
             ],
             compiler_params=pltpu.CompilerParams(
-                collective_id=0, has_side_effects=True, vmem_limit_bytes=56 * 1024 * 1024
+                collective_id=0, has_side_effects=True, vmem_limit_bytes=24 * 1024 * 1024
             ),
-        )(*operands)
+        )(*(x if x.size == 1 else pltpu.with_memory_space_constraint(x, pltpu.HBM) for x in operands))
         return jnp.swapaxes(trace_field, 1, 2), jnp.swapaxes(robin_data, 1, 2), coefficients
 
     in_specs = (

time: 43.3 us -> 40.5 us (0.935)
  local copies, waits for them, and re-layouts: 3.82 us -> 1.73 us
  Pallas kernels: 37.9 us -> 37.4 us
    unnamed x3, local copies, waits for them, and re-layouts: 3.82 us -> 1.73 us
    pallas_call x1, Pallas kernels: 37.9 us -> 37.4 us  [body(): pl.pallas_call(functools.partial(kernel, groups, peers), out_shape=(jax.S...]
where the time goes in v3:
time: 40.5 us; the launch traced here: 40.4 us
  Pallas kernels  37.4 us (92%)
  local copies, waits for them, and re-layouts  1.73 us (4%)
  between operations  1.29 us (3%)
    pallas_call x1, Pallas kernels, body(): pl.pallas_call(functools.partial(kernel, groups, peers), out_shape=(jax.S...  37.4 us
    unnamed x3, local copies, waits for them, and re-layouts  1.73 us

profile of v3, /device:TPU:0, one launch (start us, length us, event | category | flops | bytes accessed | tf_op | source)
XLA Modules:
  0.0 40.4 jit_solution(5241990629059180318)
XLA Ops:
  1.3 37.4 %shard_map.121 = (f32[1,15,1,384]{3,2,1,0:T(1,128)S(1)}, f32[1,15,1,384]{3,2,1,0:T(1,128)S(1)}, f32[1,1,64]{2,1,0:T(1,128)S(1)}) custom-call(f32[1,15,1,384]{3,2,1,0:T(1,128)} %bitcast.14, bf16[1,1,15,15,4,384]{5,4,3,2,1,0:T(4,128)(2,1)} %bitcast.13, s32[1,3,1,384]{3,2,1,0:T(1,128)} %bitcast.15, s32[1,1]{1,0:T(1,128)S(6)} %copy.18.count_hbm, ...), custom_call_target="tpu_custom_call" | custom-call | tf_op jit(solution)/shard_map/pallas_call | solution.py:394
  38.6 0.6 %copy.19 = f32[1,1,15,384]{3,1,2,0:T(1,128)} copy(f32[1,1,15,384]{3,1,2,0:T(1,128)S(1)} %bitcast.11) | data formatting | bytes 46080
  39.2 0.6 %copy.20 = f32[1,1,15,384]{3,1,2,0:T(1,128)} copy(f32[1,1,15,384]{3,1,2,0:T(1,128)S(1)} %bitcast.10) | data formatting | bytes 46080
  39.9 0.5 %copy.21 = f32[1,1,64]{2,1,0:T(1,128)} copy(f32[1,1,64]{2,1,0:T(1,128)S(1)} %get-tuple-element.17) | data formatting | bytes 512

commit v4 on v3

--- a/solution.py
+++ b/solution.py
@@ -73,6 +73,7 @@
     moved_s,
     table_s,
     folded_s,
+    shared_s,
     slots_s,
     inside_s,
     owner_s,
@@ -191,7 +192,7 @@
     eye = iota((cvec, cvec), 0) == iota((cvec, cvec), 1)
 
     fetches[5].wait()
-    lax.fori_loop(0, trace_dim, unpack, 0)
+    lax.fori_loop(0, trace_dim, unpack, 0, unroll=3)
     count = (peers - 1) + jnp.where(g > 0, peers, 0) + jnp.where(g < groups - 1, peers, 0)
 
     def apply(x):
@@ -268,6 +269,10 @@
         )
 
     def fold():
+        for a in range(trace_dim):
+            shared = pick_lanes(basis_ref[0, 0, a], slots_s[...])
+            for s in range(slots_s.shape[1] // LANES):
+                shared_s[s, a] = shared[:, s * LANES : (s + 1) * LANES]
         for k in range(kc):
             folded_s[k] = jnp.dot(
                 inverse_ref[0, 0],
@@ -278,6 +283,12 @@
 
     def relax(bx):
         trace_s[...] = sweep(trace_s[...], bx)
+
+    def prepare(t):
+        outgoing = 2.0 * robin_weight * trace_s[...] - robin_s[...]
+        sent = pick_lanes(outgoing, slots_s[...])
+        for s in range(slots_s.shape[1] // LANES):
+            robin_send[t, s] = sent[:, s * LANES : (s + 1) * LANES]
 
     def coarse(t, bx):
         residual = right_side() - bx
@@ -294,23 +305,24 @@
         def exchange(r, carry):
             send_row(t, r, as_row(coef_s[:, 0:cvec]))
             pl.when((t == 0) & (r == 0))(fold)
+            pl.when(r == 0)(lambda: prepare(t))
             wait_rows(t, r, coarse_recv_sem)
             coef_s[...] = start_s[...] - coupled(t, r)
             return carry
 
         lax.fori_loop(0, CSWEEPS, exchange, 0)
+        for s in range(slots_s.shape[1] // LANES):
+            for a in range(trace_dim):
+                moved = jnp.sum(shared_s[s, a] * coef_s[...], axis=0, keepdims=True)
+                robin_send[t, s, a : a + 1, :] += 2.0 * robin_weight * moved
+        for off in range(1, peers):
+            robin_copy(t, off).start()
         coef_out[0] = as_row(coef_s[:, 0:cvec])
         wide = jnp.concatenate([coef_s[...]] * (faces // LANES), axis=1)
         for a in range(trace_dim):
             moved_s[a : a + 1, :] = jnp.sum(basis_ref[0, 0, a] * wide, axis=0, keepdims=True)
         x = trace_s[...] + live * moved_s[...]
         trace_s[...] = x
-        outgoing = 2.0 * robin_weight * x - robin_s[...]
-        sent = pick_lanes(outgoing, slots_s[...])
-        for s in range(slots_s.shape[1] // LANES):
-            robin_send[t, s] = sent[:, s * LANES : (s + 1) * LANES]
-        for off in range(1, peers):
-            robin_copy(t, off).start()
         for a in range(trace_dim):
             trace_out[0, a] = x[a : a + 1, :]
 
@@ -413,6 +425,7 @@
                 vmem((rows, faces), f32),
                 vmem((3 * peers, 1, LANES), f32),
                 vmem((kc, cvec, cvec), f32),
+                vmem((chunks, trace_dim, cvec, LANES), f32),
                 vmem((1, chunks * LANES), jnp.int32),
                 vmem((1, faces), jnp.int32),
                 vmem((1, faces), jnp.int32),

time: 40.5 us -> 40 us (0.988)
  Pallas kernels: 37.4 us -> 36.8 us
    pallas_call x1, Pallas kernels: 37.4 us -> 36.8 us  [body(): pl.pallas_call(functools.partial(kernel, groups, peers), out_shape=(jax.S...]
where the time goes in v4:
time: 40 us; the launch traced here: 39.8 us
  Pallas kernels  36.8 us (92%)
  local copies, waits for them, and re-layouts  1.73 us (4%)
  between operations  1.29 us (3%)
    pallas_call x1, Pallas kernels, body(): pl.pallas_call(functools.partial(kernel, groups, peers), out_shape=(jax.S...  36.8 us
    unnamed x3, local copies, waits for them, and re-layouts  1.73 us

profile of v4, /device:TPU:0, one launch (start us, length us, event | category | flops | bytes accessed | tf_op | source)
XLA Modules:
  0.0 39.8 jit_solution(14623192320672615289)
XLA Ops:
  1.3 36.8 %shard_map.121 = (f32[1,15,1,384]{3,2,1,0:T(1,128)S(1)}, f32[1,15,1,384]{3,2,1,0:T(1,128)S(1)}, f32[1,1,64]{2,1,0:T(1,128)S(1)}) custom-call(f32[1,15,1,384]{3,2,1,0:T(1,128)} %bitcast.14, bf16[1,1,15,15,4,384]{5,4,3,2,1,0:T(4,128)(2,1)} %bitcast.13, s32[1,3,1,384]{3,2,1,0:T(1,128)} %bitcast.15, s32[1,1]{1,0:T(1,128)S(6)} %copy.18.count_hbm, ...), custom_call_target="tpu_custom_call" | custom-call | tf_op jit(solution)/shard_map/pallas_call | solution.py:406
  38.1 0.6 %copy.19 = f32[1,1,15,384]{3,1,2,0:T(1,128)} copy(f32[1,1,15,384]{3,1,2,0:T(1,128)S(1)} %bitcast.11) | data formatting | bytes 46080
  38.7 0.6 %copy.20 = f32[1,1,15,384]{3,1,2,0:T(1,128)} copy(f32[1,1,15,384]{3,1,2,0:T(1,128)S(1)} %bitcast.10) | data formatting | bytes 46080
  39.3 0.5 %copy.21 = f32[1,1,64]{2,1,0:T(1,128)} copy(f32[1,1,64]{2,1,0:T(1,128)S(1)} %get-tuple-element.17) | data formatting | bytes 512

commit v5 on v4

--- a/solution.py
+++ b/solution.py
@@ -78,7 +78,6 @@
     inside_s,
     owner_s,
     interface_s,
-    start_s,
     coef_s,
     coarse_send,
     coarse_recv,
@@ -299,25 +298,22 @@
                 part = part + product[:, s * LANES : (s + 1) * LANES]
         restricted = jnp.sum(part, axis=1, keepdims=True)
         start = jnp.sum(inverse_ref[0, 0] * as_row(restricted), axis=1, keepdims=True)
-        start_s[...] = jnp.broadcast_to(start, start_s.shape)
-        coef_s[...] = start_s[...]
-
-        def exchange(r, carry):
-            send_row(t, r, as_row(coef_s[:, 0:cvec]))
-            pl.when((t == 0) & (r == 0))(fold)
-            pl.when(r == 0)(lambda: prepare(t))
+        coef = start
+        for r in range(CSWEEPS):
+            send_row(t, r, as_row(coef))
+            if r == 0:
+                pl.when(t == 0)(fold)
+                prepare(t)
             wait_rows(t, r, coarse_recv_sem)
-            coef_s[...] = start_s[...] - coupled(t, r)
-            return carry
-
-        lax.fori_loop(0, CSWEEPS, exchange, 0)
+            coef = start - coupled(t, r)
+        coef_s[...] = jnp.broadcast_to(coef, coef_s.shape)
         for s in range(slots_s.shape[1] // LANES):
             for a in range(trace_dim):
                 moved = jnp.sum(shared_s[s, a] * coef_s[...], axis=0, keepdims=True)
                 robin_send[t, s, a : a + 1, :] += 2.0 * robin_weight * moved
         for off in range(1, peers):
             robin_copy(t, off).start()
-        coef_out[0] = as_row(coef_s[:, 0:cvec])
+        coef_out[0] = as_row(coef)
         wide = jnp.concatenate([coef_s[...]] * (faces // LANES), axis=1)
         for a in range(trace_dim):
             moved_s[a : a + 1, :] = jnp.sum(basis_ref[0, 0, a] * wide, axis=0, keepdims=True)
@@ -431,7 +427,6 @@
                 vmem((1, faces), jnp.int32),
                 vmem((1, faces), f32),
                 vmem((cvec, LANES), f32),
-                vmem((cvec, LANES), f32),
                 vmem((ITERS, CSWEEPS, 1, LANES), f32),
                 vmem((ITERS, CSWEEPS, 3 * peers, 1, LANES), f32),
                 vmem((ITERS, chunks, rows, LANES), f32),

time: 40 us -> 39.9 us (level)
  no operation moved by 1% of the time
where the time goes in v5:
time: 39.9 us; the launch traced here: 39.7 us
  Pallas kernels  36.7 us (92%)
  local copies, waits for them, and re-layouts  1.73 us (4%)
  between operations  1.29 us (3%)
    pallas_call x1, Pallas kernels, body(): pl.pallas_call(functools.partial(kernel, groups, peers), out_shape=(jax.S...  36.7 us
    unnamed x3, local copies, waits for them, and re-layouts  1.73 us

profile of v5, /device:TPU:0, one launch (start us, length us, event | category | flops | bytes accessed | tf_op | source)
XLA Modules:
  0.0 39.7 jit_solution(12483148368622987682)
XLA Ops:
  1.3 36.7 %shard_map.121 = (f32[1,15,1,384]{3,2,1,0:T(1,128)S(1)}, f32[1,15,1,384]{3,2,1,0:T(1,128)S(1)}, f32[1,1,64]{2,1,0:T(1,128)S(1)}) custom-call(f32[1,15,1,384]{3,2,1,0:T(1,128)} %bitcast.14, bf16[1,1,15,15,4,384]{5,4,3,2,1,0:T(4,128)(2,1)} %bitcast.13, s32[1,3,1,384]{3,2,1,0:T(1,128)} %bitcast.15, s32[1,1]{1,0:T(1,128)S(6)} %copy.18.count_hbm, ...), custom_call_target="tpu_custom_call" | custom-call | tf_op jit(solution)/shard_map/pallas_call | solution.py:402
  38.0 0.6 %copy.19 = f32[1,1,15,384]{3,1,2,0:T(1,128)} copy(f32[1,1,15,384]{3,1,2,0:T(1,128)S(1)} %bitcast.11) | data formatting | bytes 46080
  38.6 0.6 %copy.20 = f32[1,1,15,384]{3,1,2,0:T(1,128)} copy(f32[1,1,15,384]{3,1,2,0:T(1,128)S(1)} %bitcast.10) | data formatting | bytes 46080
  39.2 0.5 %copy.21 = f32[1,1,64]{2,1,0:T(1,128)} copy(f32[1,1,64]{2,1,0:T(1,128)S(1)} %get-tuple-element.17) | data formatting | bytes 512
